TPU v7x, 512 devices: a whole 4x4x16 slice. The times are simulated.
512 devices in a mesh: rep: 32 (over z, x_lo), gz: 16 (over x_hi, y, core).
Axes of the slice: x: 4 (x_hi: 2, x_lo: 2; x = x_hi * 2 + x_lo), y: 4, z: 16, core: 2. Of those that a mesh axis runs over, the one named last changes fastest.
Arguments:
- lattice_field: float32 [192, 64, 4096], P('rep', 'gz'), may hold values from -4 to 4
- langevin_noise: float32 [2, 192, 64, 4096], P(None, 'rep', 'gz'), may hold values from -5 to 5
- masses: float32 [64, 4096], P('gz'), may hold values from -2 to 2
- counts: int32 [192], replicated, may hold values from 0 to 49, as said below
- dest_slots: int32 [192], replicated, may hold values from 0 to 191, each once
- mode_bins: int32 [64, 64, 33], P('gz'), may hold values from 0 to 15, as said below
Outputs:
- resampled: float32 [192, 64, 4096], P('rep', 'gz')
- propagator: float32 [192, 16], P('rep')
Inputs may be any that keep to these rules, and one draw needn't show every extreme that they name: The counts sum to 192; in each aligned block of 6 replicas (those of one index of rep) at most 3 counts are nonzero, and exactly 3 in some block. `dest_slots`: A permutation of the 192 slots. `mode_bins`: the bin depends only on n_y^2 + n_z^2 + kx^2 with n = min(k, 64 - k), and never falls as that grows; every bin holds at least one mode.
All inputs are finite; a program needn't handle non-finite values.
Results may differ from a plain program's by a relative error of at most 0.00007.
Values sent between devices are 32-bit elements; how exact they have to be, the bound alone decides.
No kernel may reach another device: no remote copies, remote signals or barrier semaphores. Data moves between devices by JAX's collectives and lax.ppermute only.
A program may use at most 64 MiB of HBM per device.

v0:
```python
import jax
import jax.numpy as jnp
from jax import lax
from jax.sharding import PartitionSpec as P

L = 64
SWEEPS = 2
NBINS = 16
step_size = 0.1
quartic = 0.5


def with_halo(block, sides, width):
    for axis, dim in sides:
        count = lax.axis_size(axis)
        forward = [(i, i + 1) for i in range(count - 1)]
        forward.append((count - 1, 0))
        backward = [(target, source) for source, target in forward]
        low = lax.ppermute(
            lax.slice_in_dim(block, block.shape[dim] - width, None, axis=dim), axis, forward
        )
        high = lax.ppermute(lax.slice_in_dim(block, 0, width, axis=dim), axis, backward)
        block = jnp.concatenate([low, block, high], axis=dim)
    return block


def in_plane(center):
    grid = center.reshape(center.shape[0], center.shape[1], L, L)
    across = jnp.roll(grid, 1, axis=3) + jnp.roll(grid, -1, axis=3)
    return jnp.roll(center, L, axis=2) + jnp.roll(center, -L, axis=2) + across.reshape(center.shape)


def update(center, below, above, site_masses, noise_now):
    beside = below + above + in_plane(center)
    drift = 6.0 * center - beside + site_masses[None] * center + quartic * center * center * center
    return center - step_size * drift + jnp.sqrt(2.0 * step_size) * noise_now


def angle_tables(rows, columns):
    product = jnp.arange(rows)[:, None] * jnp.arange(columns)[None, :] % L
    theta = 2.0 * jnp.pi / L * product.astype(jnp.float32)
    return (jnp.cos(theta), jnp.sin(theta))


def make_weights(mode_bins):
    half = L // 2 + 1
    ordered = jnp.transpose(mode_bins, (1, 0, 2))
    wave_x = jnp.arange(half)
    weight_x = jnp.where((wave_x == 0) | (wave_x == L // 2), 1.0, 2.0).astype(jnp.float32)
    onehot = (ordered[..., None] == jnp.arange(NBINS)[None, None, None, :]).astype(jnp.float32)
    return (onehot * weight_x[None, None, :, None]).reshape(-1, NBINS)


def transform(slabs, weights):
    half = L // 2 + 1
    exact = lax.Precision.HIGHEST
    cos_half, sin_half = angle_tables(L, half)
    cos_full, sin_full = angle_tables(L, L)
    along_x = jnp.concatenate([cos_half, -sin_half], axis=1)
    count, depth = (slabs.shape[0], slabs.shape[1])
    grid = slabs.reshape(count, depth, L, L)
    first = jnp.einsum("nzyx,xk->nzyk", grid, along_x, precision=exact)
    real_x, imag_x = (first[..., :half], first[..., half:])
    real_y = jnp.einsum("qy,nzyk->nzqk", cos_full, real_x, precision=exact) + jnp.einsum(
        "qy,nzyk->nzqk", sin_full, imag_x, precision=exact
    )
    imag_y = jnp.einsum("qy,nzyk->nzqk", cos_full, imag_x, precision=exact) - jnp.einsum(
        "qy,nzyk->nzqk", sin_full, real_x, precision=exact
    )
    merged = jnp.concatenate([real_y, imag_y], axis=3).reshape(count, depth, L * 2 * half)
    block = lax.all_to_all(merged, "gz", split_axis=2, concat_axis=1, tiled=True)
    items = block.shape[0]
    pencil = block.reshape(items, L, -1, 2 * half)
    real_p = pencil[..., :half]
    imag_p = pencil[..., half:]
    real_z = jnp.einsum("pz,mzqk->mpqk", cos_full, real_p, precision=exact) + jnp.einsum(
        "pz,mzqk->mpqk", sin_full, imag_p, precision=exact
    )
    imag_z = jnp.einsum("pz,mzqk->mpqk", cos_full, imag_p, precision=exact) - jnp.einsum(
        "pz,mzqk->mpqk", sin_full, real_p, precision=exact
    )
    power = real_z * real_z + imag_z * imag_z
    binned = jnp.dot(power.reshape(items, -1), weights, precision=exact)
    binned_total, weight_total = lax.psum((binned, jnp.sum(weights, axis=0)), "gz")
    return binned_total / (float(L**3) * weight_total)


def local(lattice_field, langevin_noise, masses, counts, dest_slots, mode_bins):
    local_count = lattice_field.shape[0]
    weights = make_weights(mode_bins)
    swept = lattice_field
    for turn in range(SWEEPS):
        padded = with_halo(swept, (("gz", 1),), 1)
        swept = update(padded[:, 1:-1], padded[:, :-2], padded[:, 2:], masses, langevin_noise[turn])
    base = lax.axis_index("rep") * local_count
    ends = jnp.cumsum(counts)
    position = jnp.argsort(dest_slots)
    mine_position = lax.dynamic_slice_in_dim(position, base, local_count)
    mine_source = jnp.sum((ends[None, :] <= mine_position[:, None]).astype(jnp.int32), axis=1)
    empty = jnp.zeros_like(swept)
    piece = lax.all_gather(swept, "rep", axis=0, tiled=True)
    found = (mine_source >= 0) & (mine_source < piece.shape[0])
    chosen = jnp.take(piece, jnp.clip(mine_source, 0, piece.shape[0] - 1), axis=0)
    resampled = jnp.where(found[:, None, None], chosen, empty)
    propagator = transform(resampled, weights)
    return (resampled, propagator)


def solution(mesh):
    in_specs = (
        P("rep", "gz", None),
        P(None, "rep", "gz", None),
        P("gz", None),
        P(),
        P(),
        P("gz", None, None),
    )
    out_specs = (P("rep", "gz", None), P("rep", None))
    return jax.shard_map(local, mesh=mesh, in_specs=in_specs, out_specs=out_specs, check_vma=False)
```

profile of v0, /device:TPU:38, one launch (start us, length us, event | category | flops | bytes accessed | tf_op | source)
XLA Modules:
  0.0 452.3 jit_solution(2166895266252879648)
XLA Ops:
  8.5 1.9 collective-permute-start
  10.4 7.3 %collective-permute-start.1 = (f32[6,1,4096]{2,1,0:T(1,128)S(1)}, f32[6,1,4096]{2,1,0:T(1,128)S(1)}, u32[]{:S(2)}, u32[]{:S(2)}) collective-permute-start(f32[6,1,4096]{2,1,0:T(1,128)S(1)} %get-tuple-element.27), channel_id=1, source_target_pairs={{1,0},{2,1},{3,2},{4,3},{5,4},{6,5},{7,6},{8,7},{9,8},{10,9},{11,1... | collective-permute-start | bytes 294920 | tf_op jit(solution)/shard_map/ppermute | solution.py:22
  17.7 1.4 reshape.93
  23.0 1.8 fusion.23
  26.9 1.9 collective-permute-start.2
  28.8 7.4 %collective-permute-start.3 = (f32[6,1,4096]{2,1,0:T(1,128)}, f32[6,1,4096]{2,1,0:T(1,128)S(1)}, u32[]{:S(2)}, u32[]{:S(2)}) collective-permute-start(f32[6,1,4096]{2,1,0:T(1,128)} %get-tuple-element.21), channel_id=1, source_target_pairs={{1,0},{2,1},{3,2},{4,3},{5,4},{6,5},{7,6},{8,7},{9,8},{10,9},{11,1... | collective-permute-start | bytes 294920 | tf_op jit(solution)/shard_map/ppermute | solution.py:22
  37.1 1.5 collective-permute-done.3
  38.6 1.6 fusion.27
  41.3 3.2 sort.17
  45.3 281.6 %all-gather.2.cloned.1.call-done = f32[192,4,4096]{2,1,0:T(4,128)} async-done(((f32[6,4,4096]{2,1,0:T(4,128)}), f32[192,4,4096]{2,1,0:T(4,128)}) %all-gather.2.cloned.1.call-update) | async-done | bytes 12582928 | tf_op jit(solution)/shard_map/all_gather | solution.py:101
  326.9 5.4 %gather_fusion = f32[6,4,4096]{2,1,0:T(4,128)S(1)} fusion(f32[192,4,4096]{2,1,0:T(4,128)} %all-gather.2.cloned.1.call-done, s32[1024]{0:T(1024)S(1)} %pad_clamp_fusion), kind=kCustom, calls=%fused_computation | custom fusion | bytes 786456 | tf_op jit(solution)/shard_map/jit(_take)/gather | solution.py:103
  333.5 1.4 fusion.14
  335.0 1.6 fusion.10
  336.6 1.6 fusion.5
  338.2 1.4 fusion.4
  339.7 9.3 %copy.65 = f32[6,4,64,66]{0,1,3,2:T(4,128)} copy(f32[6,4,64,66]{2,3,1,0:T(8,128)S(1)} %pad_maximum_fusion) | data formatting | bytes 811008 | tf_op jit(solution)/shard_map/reshape | solution.py:70
  349.0 12.4 %reshape.110 = f32[16,1,6336]{2,1,0:T(1,128)} reshape(f32[4224,4,6]{2,1,0:T(4,128)} %bitcast.64) | data formatting | bytes 811008
  361.4 7.3 %all-to-all-start = ((f32[16,1,6336]{2,1,0:T(1,128)}), f32[16,1,6336]{2,1,0:T(1,128)S(1)}, u32[]{:S(2)}, u32[]{:S(2)}) async-start(f32[16,1,6336]{2,1,0:T(1,128)} %reshape.110), calls=%async_computation | async-start | bytes 819200 | tf_op jit(solution)/shard_map/all_to_all | solution.py:71
  369.6 7.4 %all-to-all-done = f32[16,1,6336]{2,1,0:T(1,128)S(1)} async-done(((f32[16,1,6336]{2,1,0:T(1,128)}), f32[16,1,6336]{2,1,0:T(1,128)S(1)}, u32[]{:S(2)}, u32[]{:S(2)}) %all-to-all-start) | async-done | bytes 405536 | tf_op jit(solution)/shard_map/all_to_all | solution.py:71
  377.5 1.6 reduce.2
  379.1 15.2 %reshape.111 = f32[4224,4,6]{2,1,0:T(4,128)} reshape(f32[16,6336]{1,0:T(8,128)S(1)} %reduce.2) | data formatting | bytes 811008
  394.3 7.6 %copy.51 = f32[6,4,16,264]{3,1,2,0:T(4,128)S(1)} copy(f32[6,4,16,264]{0,1,3,2:T(4,128)} %bitcast.65) | data formatting | bytes 811008 | tf_op jit(solution)/shard_map/all_to_all | solution.py:71
  406.4 1.6 convolution_bitcast_fusion
  407.9 36.9 %all-reduce.1 = (f32[6,16]{1,0:T(8,128)S(1)}, f32[16]{0:T(128)S(1)}) all-reduce(f32[6,16]{1,0:T(8,128)S(1)} %convolution_bitcast_fusion, f32[16]{0:T(128)S(1)} %select_reduce_fusion), channel_id=1, replica_groups=mesh['rep'=32,'gz'=16] {'gz'}, use_global_device_ids=true, to_apply=%region_4.5 | all-reduce | flops 112 | bytes 896 | tf_op jit(solution)/shard_map/psum | solution.py:84
  (71 shorter events, 17.8 us)
Async XLA Ops:
  7.2 319.8 %all-gather.2.cloned.1.call-start = ((), (), s32[]{:S(2)}) async-start(), calls=%async_computation.1 | async-start | bytes 12976128 | tf_op jit(solution)/shard_map/all_gather | solution.py:101
  8.5 13.6 %collective-permute-start = (f32[6,1,4096]{2,1,0:T(1,128)S(1)}, f32[6,1,4096]{2,1,0:T(1,128)S(1)}, u32[]{:S(2)}, u32[]{:S(2)}) collective-permute-start(f32[6,1,4096]{2,1,0:T(1,128)S(1)} %get-tuple-element.26), channel_id=1, source_target_pairs={{0,1},{1,2},{2,3},{3,4},{4,5},{5,6},{6,7},{7,8},{8,9},{9,10},{10,1... | collective-permute-start | bytes 294920 | tf_op jit(solution)/shard_map/ppermute | solution.py:19
  10.4 11.7 %collective-permute-start.1 = (f32[6,1,4096]{2,1,0:T(1,128)S(1)}, f32[6,1,4096]{2,1,0:T(1,128)S(1)}, u32[]{:S(2)}, u32[]{:S(2)}) collective-permute-start(f32[6,1,4096]{2,1,0:T(1,128)S(1)} %get-tuple-element.27), channel_id=1, source_target_pairs={{1,0},{2,1},{3,2},{4,3},{5,4},{6,5},{7,6},{8,7},{9,8},{10,9},{11,1... | collective-permute-start | bytes 294920 | tf_op jit(solution)/shard_map/ppermute | solution.py:22
  19.4 1.0 copy-start
  21.8 1.1 copy-start.1
  22.2 0.6 copy-start.4
  22.2 0.7 copy-start.5
  26.9 10.2 %collective-permute-start.2 = (f32[6,1,4096]{2,1,0:T(1,128)}, f32[6,1,4096]{2,1,0:T(1,128)S(1)}, u32[]{:S(2)}, u32[]{:S(2)}) collective-permute-start(f32[6,1,4096]{2,1,0:T(1,128)} %get-tuple-element.20), channel_id=1, source_target_pairs={{0,1},{1,2},{2,3},{3,4},{4,5},{5,6},{6,7},{7,8},{8,9},{9,10},{10,1... | collective-permute-start | bytes 294920 | tf_op jit(solution)/shard_map/ppermute | solution.py:19
  28.8 9.8 %collective-permute-start.3 = (f32[6,1,4096]{2,1,0:T(1,128)}, f32[6,1,4096]{2,1,0:T(1,128)S(1)}, u32[]{:S(2)}, u32[]{:S(2)}) collective-permute-start(f32[6,1,4096]{2,1,0:T(1,128)} %get-tuple-element.21), channel_id=1, source_target_pairs={{1,0},{2,1},{3,2},{4,3},{5,4},{6,5},{7,6},{8,7},{9,8},{10,9},{11,1... | collective-permute-start | bytes 294920 | tf_op jit(solution)/shard_map/ppermute | solution.py:22
  36.8 1.9 copy-start.3
  38.6 1.6 copy-start.2
  38.6 1.8 copy-start.6
  40.2 1.1 copy-start.7
  361.4 15.5 %all-to-all-start = ((f32[16,1,6336]{2,1,0:T(1,128)}), f32[16,1,6336]{2,1,0:T(1,128)S(1)}, u32[]{:S(2)}, u32[]{:S(2)}) async-start(f32[16,1,6336]{2,1,0:T(1,128)} %reshape.110), calls=%async_computation | async-start | bytes 819200 | tf_op jit(solution)/shard_map/all_to_all | solution.py:71
Sparse Core Ops, SparseCore 0:
  40.3 286.5 all-gather.1
where the time goes:
time: 453 us; the launch traced here: 452 us
  waiting for transfers between devices  290 us (64%)
  local copies, waits for them, and re-layouts  61.9 us (14%)
  blocking collectives  36.9 us (8%)
  starting transfers between devices  25.8 us (6%)
  between operations  14.4 us (3%)
  other arithmetic  11.6 us (3%)
  matrix products  11.2 us (2%)
    all_gather x1, waiting for transfers between devices, local(): piece = lax.all_gather(swept, 'rep', axis=0, tiled=True)  282 us
    psum x1, blocking collectives, transform(): lax.psum((binned, jnp.sum(weights, axis=0)), 'gz')  36.9 us
    unnamed x20, local copies, waits for them, and re-layouts  29.8 us
    ppermute x2, starting transfers between devices, with_halo(): lax.ppermute(lax.slice_in_dim(block, 0, width, axis=dim), axis, backward)  14.7 us
    reshape x1, local copies, waits for them, and re-layouts, transform(): jnp.concatenate([real_y, imag_y], axis=3)  9.27 us
  transfers between devices with their start and end apart: 6, of which 3 were waited for; matrix products, arithmetic and copies ran while one was open for 2% of the time, Pallas kernels for 0%

commit v1 on v0

--- a/solution.py
+++ b/solution.py
@@ -68,7 +68,10 @@
         "qy,nzyk->nzqk", sin_full, real_x, precision=exact
     )
     merged = jnp.concatenate([real_y, imag_y], axis=3).reshape(count, depth, L * 2 * half)
-    block = lax.all_to_all(merged, "gz", split_axis=2, concat_axis=1, tiled=True)
+    block = jnp.concatenate(
+        lax.all_to_all(jnp.stack(jnp.split(merged, lax.axis_size("gz"), axis=2)), "gz", 0, 0),
+        axis=1,
+    )
     items = block.shape[0]
     pencil = block.reshape(items, L, -1, 2 * half)
     real_p = pencil[..., :half]

time: 453 us -> 420 us (0.927)
  local copies, waits for them, and re-layouts: 61.9 us -> 28.9 us
    unnamed x20 -> x33, local copies, waits for them, and re-layouts: 29.8 us -> 12.5 us
    reshape x1, local copies, waits for them, and re-layouts: 9.27 us -> 0.59 us  [transform(): jnp.concatenate([real_y, imag_y], axis=3)]
    all_to_all x2 -> x0, local copies, waits for them, and re-layouts: 8.1 us -> none  [transform(): lax.all_to_all(merged, 'gz', split_axis=2, concat_axis=1, tiled=True)]
where the time goes in v1:
time: 420 us
  waiting for transfers between devices  292 us (70%)
  blocking collectives  36.9 us (9%)
  local copies, waits for them, and re-layouts  28.9 us (7%)
  starting transfers between devices  25.8 us (6%)
  between operations  14.4 us (3%)
  matrix products  11.2 us (3%)
  other arithmetic  10 us (2%)
    all_gather x1, waiting for transfers between devices, local(): piece = lax.all_gather(swept, 'rep', axis=0, tiled=True)  282 us
    psum x1, blocking collectives, transform(): lax.psum((binned, jnp.sum(weights, axis=0)), 'gz')  36.9 us
    ppermute x2, starting transfers between devices, with_halo(): lax.ppermute(lax.slice_in_dim(block, 0, width, axis=dim), axis, backward)  14.7 us
    unnamed x33, local copies, waits for them, and re-layouts  12.5 us
    all_to_all x1, waiting for transfers between devices, transform(): lax.all_to_all(jnp.stack(jnp.split(merged, lax.axis_size('gz'), axis=2)),...  9.29 us
  transfers between devices with their start and end apart: 6, of which 3 were waited for; matrix products, arithmetic and copies ran while one was open for 2% of the time, Pallas kernels for 0%

profile of v1, /device:TPU:38, one launch (start us, length us, event | category | flops | bytes accessed | tf_op | source)
XLA Modules:
  0.0 419.7 jit_solution(14231684890054128430)
XLA Ops:
  7.2 1.3 fusion.140
  8.5 1.9 collective-permute-start
  10.4 7.3 %collective-permute-start.1 = (f32[6,1,4096]{2,1,0:T(1,128)S(1)}, f32[6,1,4096]{2,1,0:T(1,128)S(1)}, u32[]{:S(2)}, u32[]{:S(2)}) collective-permute-start(f32[6,1,4096]{2,1,0:T(1,128)S(1)} %get-tuple-element.27), channel_id=1, source_target_pairs={{1,0},{2,1},{3,2},{4,3},{5,4},{6,5},{7,6},{8,7},{9,8},{10,9},{11,1... | collective-permute-start | bytes 294920 | tf_op jit(solution)/shard_map/ppermute | solution.py:22
  17.7 1.4 reshape.92
  23.0 1.8 fusion.23
  26.0 0.8 fusion.137
  26.9 1.9 collective-permute-start.2
  28.8 7.4 %collective-permute-start.3 = (f32[6,1,4096]{2,1,0:T(1,128)}, f32[6,1,4096]{2,1,0:T(1,128)S(1)}, u32[]{:S(2)}, u32[]{:S(2)}) collective-permute-start(f32[6,1,4096]{2,1,0:T(1,128)} %get-tuple-element.21), channel_id=1, source_target_pairs={{1,0},{2,1},{3,2},{4,3},{5,4},{6,5},{7,6},{8,7},{9,8},{10,9},{11,1... | collective-permute-start | bytes 294920 | tf_op jit(solution)/shard_map/ppermute | solution.py:22
  37.1 1.5 collective-permute-done.3
  38.6 1.6 fusion.27
  41.3 3.2 sort.17
  45.3 281.6 %all-gather.2.cloned.1.call-done = f32[192,4,4096]{2,1,0:T(4,128)} async-done(((f32[6,4,4096]{2,1,0:T(4,128)}), f32[192,4,4096]{2,1,0:T(4,128)}) %all-gather.2.cloned.1.call-update) | async-done | bytes 12582928 | tf_op jit(solution)/shard_map/all_gather | solution.py:104
  326.9 5.4 %gather_fusion = f32[6,4,4096]{2,1,0:T(4,128)S(1)} fusion(f32[192,4,4096]{2,1,0:T(4,128)} %all-gather.2.cloned.1.call-done, s32[1024]{0:T(1024)S(1)} %pad_clamp_fusion), kind=kCustom, calls=%fused_computation | custom fusion | bytes 786456 | tf_op jit(solution)/shard_map/jit(_take)/gather | solution.py:106
  332.7 0.8 fusion.7
  333.6 1.4 fusion.14
  335.0 1.6 fusion.10
  336.6 1.6 fusion.5
  338.2 1.4 fusion.4
  351.7 7.3 %all-to-all-start = ((f32[16,6,4,264]{3,2,1,0:T(4,128)}), f32[16,6,4,264]{3,2,1,0:T(4,128)S(1)}, u32[]{:S(2)}, u32[]{:S(2)}) async-start(f32[16,6,4,264]{3,2,1,0:T(4,128)} %fusion.42), calls=%async_computation | async-start | bytes 1179648 | tf_op jit(solution)/shard_map/all_to_all | solution.py:72
  359.0 0.9 select_select_fusion
  359.9 9.3 %all-to-all-done = f32[16,6,4,264]{3,2,1,0:T(4,128)S(1)} async-done(((f32[16,6,4,264]{3,2,1,0:T(4,128)}), f32[16,6,4,264]{3,2,1,0:T(4,128)S(1)}, u32[]{:S(2)}, u32[]{:S(2)}) %all-to-all-start) | async-done | bytes 405536 | tf_op jit(solution)/shard_map/all_to_all | solution.py:72
  372.3 0.7 fusion.3
  373.7 1.6 convolution_bitcast_fusion
  375.3 36.9 %all-reduce.1 = (f32[6,16]{1,0:T(8,128)S(1)}, f32[16]{0:T(128)S(1)}) all-reduce(f32[6,16]{1,0:T(8,128)S(1)} %convolution_bitcast_fusion, f32[16]{0:T(128)S(1)} %select_reduce_fusion), channel_id=1, replica_groups=mesh['rep'=32,'gz'=16] {'gz'}, use_global_device_ids=true, to_apply=%region_4.5 | all-reduce | flops 112 | bytes 896 | tf_op jit(solution)/shard_map/psum | solution.py:87
  (84 shorter events, 24.7 us)
Async XLA Ops:
  7.2 319.8 %all-gather.2.cloned.1.call-start = ((), (), s32[]{:S(2)}) async-start(), calls=%async_computation.1 | async-start | bytes 12976128 | tf_op jit(solution)/shard_map/all_gather | solution.py:104
  8.5 13.6 %collective-permute-start = (f32[6,1,4096]{2,1,0:T(1,128)S(1)}, f32[6,1,4096]{2,1,0:T(1,128)S(1)}, u32[]{:S(2)}, u32[]{:S(2)}) collective-permute-start(f32[6,1,4096]{2,1,0:T(1,128)S(1)} %get-tuple-element.26), channel_id=1, source_target_pairs={{0,1},{1,2},{2,3},{3,4},{4,5},{5,6},{6,7},{7,8},{8,9},{9,10},{10,1... | collective-permute-start | bytes 294920 | tf_op jit(solution)/shard_map/ppermute | solution.py:19
  10.4 11.7 %collective-permute-start.1 = (f32[6,1,4096]{2,1,0:T(1,128)S(1)}, f32[6,1,4096]{2,1,0:T(1,128)S(1)}, u32[]{:S(2)}, u32[]{:S(2)}) collective-permute-start(f32[6,1,4096]{2,1,0:T(1,128)S(1)} %get-tuple-element.27), channel_id=1, source_target_pairs={{1,0},{2,1},{3,2},{4,3},{5,4},{6,5},{7,6},{8,7},{9,8},{10,9},{11,1... | collective-permute-start | bytes 294920 | tf_op jit(solution)/shard_map/ppermute | solution.py:22
  19.4 1.0 copy-start
  21.8 1.1 copy-start.1
  22.2 0.6 copy-start.4
  22.2 0.7 copy-start.5
  26.9 10.2 %collective-permute-start.2 = (f32[6,1,4096]{2,1,0:T(1,128)}, f32[6,1,4096]{2,1,0:T(1,128)S(1)}, u32[]{:S(2)}, u32[]{:S(2)}) collective-permute-start(f32[6,1,4096]{2,1,0:T(1,128)} %get-tuple-element.20), channel_id=1, source_target_pairs={{0,1},{1,2},{2,3},{3,4},{4,5},{5,6},{6,7},{7,8},{8,9},{9,10},{10,1... | collective-permute-start | bytes 294920 | tf_op jit(solution)/shard_map/ppermute | solution.py:19
  28.8 9.8 %collective-permute-start.3 = (f32[6,1,4096]{2,1,0:T(1,128)}, f32[6,1,4096]{2,1,0:T(1,128)S(1)}, u32[]{:S(2)}, u32[]{:S(2)}) collective-permute-start(f32[6,1,4096]{2,1,0:T(1,128)} %get-tuple-element.21), channel_id=1, source_target_pairs={{1,0},{2,1},{3,2},{4,3},{5,4},{6,5},{7,6},{8,7},{9,8},{10,9},{11,1... | collective-permute-start | bytes 294920 | tf_op jit(solution)/shard_map/ppermute | solution.py:22
  36.8 1.9 copy-start.3
  38.6 1.6 copy-start.2
  38.6 1.8 copy-start.6
  40.2 1.1 copy-start.7
  351.7 17.5 %all-to-all-start = ((f32[16,6,4,264]{3,2,1,0:T(4,128)}), f32[16,6,4,264]{3,2,1,0:T(4,128)S(1)}, u32[]{:S(2)}, u32[]{:S(2)}) async-start(f32[16,6,4,264]{3,2,1,0:T(4,128)} %fusion.42), calls=%async_computation | async-start | bytes 1179648 | tf_op jit(solution)/shard_map/all_to_all | solution.py:72
Sparse Core Ops, SparseCore 0:
  40.3 286.5 all-gather.1
